TPU v7x, 32 devices: a whole 2x2x4 slice. The times are simulated.
32 devices in a mesh: dp: 16 (over z, y, x), mlp: 2 (over core).
Axes of the slice: x: 2, y: 2, z: 4, core: 2. Of those that a mesh axis runs over, the one named last changes fastest.
Arguments:
- tokens: bfloat16 [64, 197, 768], P(('dp', 'mlp')), may hold values from -6 to 6
- cotangent: bfloat16 [64, 197, 768], P(('dp', 'mlp')), may hold values from -6 to 6
- prompts: float32 [2, 50, 768], P(None, None, 'mlp'), may hold values from -6 to 6
- first_moment: float32 [2, 50, 768], P(None, None, 'mlp'), may hold values from -0.005859375 to 0.005859375
- second_moment: float32 [2, 50, 768], P(None, None, 'mlp'), may hold values from 1.3020833e-08 to 5.2083333e-08
- norm_params: float32 [2, 4, 768], replicated, may hold values from -1.2 to 1.9, as said below
- bias_rows: float32 [2, 4, 768], replicated, may hold values from -1.5 to 1.5
- qkv_weight: bfloat16 [2, 768, 2304], replicated, may hold values from -0.21875 to 0.21875
- out_weight: bfloat16 [2, 768, 768], replicated, may hold values from -0.625 to 0.625
- up_weight: bfloat16 [2, 768, 3072], P(None, None, 'mlp'), may hold values from -0.21875 to 0.21875
- up_bias: float32 [2, 3072], P(None, 'mlp'), may hold values from -1.5 to 1.5
- down_weight: bfloat16 [2, 3072, 768], P(None, 'mlp'), may hold values from -0.109375 to 0.109375
Outputs:
- activations: bfloat16 [64, 197, 768], P(('dp', 'mlp'))
- input_grad: float32 [64, 197, 768], P(('dp', 'mlp'))
- prompt_grad: float32 [2, 50, 768], P(None, None, 'mlp')
- grad_norm: float32 [], replicated
- new_first: float32 [2, 50, 768], P(None, None, 'mlp')
- new_second: float32 [2, 50, 768], P(None, None, 'mlp')
- new_prompts: float32 [2, 50, 768], P(None, None, 'mlp')
Inputs may be any that keep to these rules, and one draw needn't show every extreme that they name: `norm_params`: gains in rows 0 and 2 of the middle dimension are positive.
All inputs are finite; a program needn't handle non-finite values.
Results may differ from a plain program's by a relative error of at most 0.025.
Values may be sent and summed in bfloat16 or wider, within the bound.
A program may use at most 128 MiB of HBM per device.

v0:
```python
import functools

import jax
import jax.numpy as jnp
from jax import lax
from jax.experimental import pallas as pl
from jax.experimental.pallas import tpu as pltpu
from jax.sharding import PartitionSpec as P

HEADS = 12
STEP = 10
MESH = pl.DeviceIdType.MESH
VMEM = pltpu.VMEM
DMA = pltpu.SemaphoreType.DMA
BF16 = jnp.bfloat16
F32 = jnp.float32

norm_eps = 1e-06
clip_limit = 1.0
beta_one = 0.9
beta_two = 0.999
learn_rate = 1.5
weight_decay = 0.05
adam_eps = 1e-08
LOG2E = 1.4426950408889634


def up_to(value, step):
    return -(-value // step) * step


def mm(left, right):
    return jnp.dot(left, right, preferred_element_type=F32)


def mm_nt(left, right):
    return lax.dot_general(left, right, (((1,), (1,)), ((), ())), preferred_element_type=F32)


def mm_tn(left, right):
    return lax.dot_general(left, right, (((0,), (0,)), ((), ())), preferred_element_type=F32)


def rows_loop(count, step, body, unroll=1):
    def one(i, carry):
        body(pl.multiple_of(i * step, step))
        return carry

    lax.fori_loop(0, count // step, one, 0, unroll=unroll)


def main_kernel(
    dims,
    tok_hbm,
    cot_hbm,
    prompts_hbm,
    first_hbm,
    second_hbm,
    norms_hbm,
    bias_hbm,
    qkv_hbm,
    out_hbm,
    up_hbm,
    ub_hbm,
    dn_hbm,
    tok_nat,
    stage_nat,
    grad_nat,
    norm_s,
    first_nat,
    second_nat,
    prompt_nat,
    cot_nat,
    prom_nat,
    norms,
    bias,
    w_qkv,
    w_out,
    w_up,
    ub,
    w_dn,
    seq,
    hid,
    acc,
    wide,
    x16,
    xh1,
    xh2,
    inv_s,
    q_s,
    k_s,
    v_s,
    e_s,
    ri_s,
    o_s,
    gp_s,
    part_h,
    slot_b,
    slot_c,
    fin,
    sq_out,
    sq_in,
    local_sem,
    weight_sem,
    push_sem,
    push_w_sem,
    sem_b,
    sem_c,
    sem_d,
    sem_e,
):
    B, T, D, L, PN, TK, S, TQ, FH, G, R = dims
    H = HEADS
    HD = D // H
    C = 768
    NJ = D // 128
    HJ = NJ // 2
    PB = 16
    core = lax.axis_index("mlp")
    other = 1 - core
    me = lax.axis_index("dp")
    g, r = lax.rem(me, G), me // G
    half = D // 2

    def member(k):
        return lax.rem(g + k, G)

    def rank(k):
        return lax.rem(r + k, R)

    around = [(k, c) for k in range(G) for c in range(2)][1:]

    def neighbour(k, c):
        return {"dp": r * G + member(k), "mlp": lax.rem(core + c, 2)}

    barrier = pltpu.get_barrier_semaphore()
    for k, c in around:
        pl.semaphore_signal(barrier, inc=1, device_id=neighbour(k, c), device_id_type=MESH)

    def greet(k, carry):
        pl.semaphore_signal(
            barrier, inc=1, device_id={"dp": rank(k) * G + g}, device_id_type=MESH
        )
        return carry

    lax.fori_loop(1, R, greet, 0)

    def columns(j):
        return slice(128 * j, 128 * (j + 1))

    def local(i, src, dst):
        return pltpu.make_async_copy(src, dst, local_sem.at[i])

    def copy_tok(j):
        return local(j, tok_hbm.at[:, :, columns(j)], tok_nat.at[j])

    def copy_cot(j):
        return local(NJ + j, cot_hbm.at[:, :, columns(j)], cot_nat.at[j])

    def copy_prom(j):
        return local(2 * NJ + j, prompts_hbm.at[:, :, columns(j)], prom_nat.at[core * HJ + j])

    def copy_moment(i, j):
        src = (first_hbm, second_hbm)[i]
        return local(
            2 * NJ + (i + 1) * HJ + j, src.at[:, :, columns(j)], (first_nat, second_nat)[i].at[j]
        )

    def copy_small(i):
        src, dst = ((norms_hbm, norms), (bias_hbm, bias), (ub_hbm, ub.at[0]))[i]
        return local(2 * NJ + 3 * HJ + i, src, dst)

    def copy_weight(l, i):
        src, dst = (
            (qkv_hbm.at[l], w_qkv.at[l]),
            (out_hbm.at[l], w_out.at[l]),
            (up_hbm.at[l], w_up.at[l, 0]),
            (dn_hbm.at[l], w_dn.at[l, 0]),
        )[i]
        return pltpu.make_async_copy(src, dst, weight_sem.at[l, i])

    def push(src, dst, send_at, recv_at):
        return pltpu.make_async_remote_copy(
            src_ref=src,
            dst_ref=dst,
            send_sem=send_at,
            recv_sem=recv_at,
            device_id={"mlp": other},
            device_id_type=MESH,
        )

    def push_prom(j):
        return push(
            prompts_hbm.at[:, :, columns(j)],
            prom_nat.at[core * HJ + j],
            push_sem.at[0, j],
            push_sem.at[1, j],
        )

    def push_ub():
        return push(ub_hbm, ub.at[1], push_sem.at[0, HJ], push_sem.at[1, HJ])

    def push_weight(l, i):
        src, dst = ((up_hbm.at[l], w_up.at[l, 1]), (dn_hbm.at[l], w_dn.at[l, 1]))[i]
        return push(src, dst, push_w_sem.at[l, 0, i], push_w_sem.at[l, 1, i])

    for j in range(NJ):
        copy_tok(j).start()
    for j in range(HJ):
        copy_prom(j).start()
    copy_small(0).start()
    copy_small(1).start()
    copy_weight(0, 0).start()
    pl.semaphore_wait(barrier, len(around) + R - 1)
    for j in range(HJ):
        push_prom(j).start()
    push_ub().start()
    push_weight(0, 0).start()
    push_weight(0, 1).start()

    tok_v = tok_nat.reshape(NJ, T * B, 128)
    cot_v = cot_nat.reshape(NJ, T * B, 128)
    stage_v = stage_nat.reshape(NJ, T * B, 128)
    prom_v = prom_nat.reshape(NJ, PN * L, 128)

    lane = lax.broadcasted_iota(jnp.int32, (1, S), 1)
    valid = (lane < T) | ((lane >= TK) & (lane < TK + PN))
    key_bias = jnp.where(valid, 0.0, -1e30).astype(F32)
    even_q = lax.broadcasted_iota(jnp.int32, (TQ, 2 * HD), 1) < HD
    even_k = lax.broadcasted_iota(jnp.int32, (S, 2 * HD), 1) < HD
    SH = S // 2
    even_h = lax.broadcasted_iota(jnp.int32, (SH, 2 * HD), 1) < HD
    low_lane = lax.broadcasted_iota(jnp.int32, (TQ, S), 1) < SH
    scale = HD**-0.5

    def spread(src_v, store):
        for j in range(NJ):
            stage_v[j] = src_v[j].astype(F32)
        for b in range(B):
            for j in range(NJ):
                store(b, slice(128 * j, 128 * (j + 1)), stage_v[j, pl.ds(b, T, stride=B), :])

    for b in range(B):
        seq[b, TK - 8 :, :] = jnp.zeros((S - TK + 8, D), F32)
    for j in range(NJ):
        copy_tok(j).wait()

    def store_tok(b, cols, rows):
        seq[b, 0:T, cols] = rows

    spread(tok_v, store_tok)
    copy_small(0).wait()
    copy_small(1).wait()
    for j in range(HJ):
        copy_prom(j).wait()
        push_prom(j).wait()

    def norm_rows(x):
        mean = jnp.mean(x, axis=-1, keepdims=True)
        centre = x - mean
        spread_ = jnp.mean(centre * centre, axis=-1, keepdims=True)
        inv = lax.rsqrt(spread_ + norm_eps)
        return centre * inv, inv

    def ln_back(dy, xh, inv, gain):
        gdy = dy * gain
        a = jnp.mean(gdy, axis=-1, keepdims=True)
        c = jnp.mean(gdy * xh, axis=-1, keepdims=True)
        return inv * (gdy - a - xh * c)

    def attend_forward(l):
        def pair(i, carry):
            b = i // (H // 2)
            hp = i % (H // 2)
            sl = pl.ds(pl.multiple_of(hp * 2 * HD, 2 * HD), 2 * HD)
            qr = pl.ds(pl.multiple_of(b * TQ, 16), TQ)
            kr = pl.ds(pl.multiple_of(b * S, 16), S)
            q = q_s[l, qr, sl]
            k = k_s[l, kr, sl]
            v = v_s[l, kr, sl]
            sums = []
            for h in range(2):
                here = even_k if h == 0 else jnp.logical_not(even_k)
                s = mm_nt(q, jnp.where(here, k, jnp.zeros_like(k))) + key_bias
                top = jnp.max(s, axis=1, keepdims=True)
                e = jnp.exp2((s - top) * (LOG2E * scale)).astype(BF16)
                e_s[l, b, hp * 2 + h] = e
                sums.append(mm(e, jnp.where(here, v, jnp.ones_like(v))))
            top_part = jnp.where(even_q, sums[0], sums[1])
            total = jnp.where(even_q, sums[1], sums[0])
            inv = pltpu.roll(1.0 / total, HD, 1)
            ri_s[l, qr, sl] = inv.astype(BF16)
            o_s[l, qr, sl] = (top_part * inv).astype(BF16)
            return carry

        lax.fori_loop(0, B * H // 2, pair, 0, unroll=6)

    def back_half(l, b, hp, part, first):
        at = pl.multiple_of(hp * 2 * HD, 2 * HD)
        sl = pl.ds(at, 2 * HD)
        qr = pl.ds(pl.multiple_of(b * TQ, 16), TQ)
        kr = pl.ds(pl.multiple_of(b * S + part * SH, 16), SH)
        v = v_s[l, kr, sl]
        spare = pl.ds(pl.multiple_of((b * (H // 2) + hp) * S, 128), TQ)
        if first:
            do = x16[qr, sl].astype(F32) * ri_s[l, qr, sl].astype(F32)
            prod = do * o_s[l, qr, sl].astype(F32)
            d0 = jnp.sum(jnp.where(even_q, prod, 0.0), axis=1, keepdims=True)
            d1 = jnp.sum(jnp.where(even_q, 0.0, prod), axis=1, keepdims=True)
            do16 = do.astype(BF16)
            q_t = q_s[l, qr, sl].T
            do_t = do16.T
            x16[qr, sl] = do16
            gp_s[l, 0 : 2 * HD, spare] = q_t
            gp_s[l, 2 * HD : 4 * HD, spare] = do_t
            acc[qr, sl] = jnp.where(even_q, d0, d1)
        else:
            do16 = x16[qr, sl]
            q_t = gp_s[l, 0 : 2 * HD, spare]
            do_t = gp_s[l, 2 * HD : 4 * HD, spare]
            both = acc[qr, sl]
            d0, d1 = both[:, 0:1], both[:, HD : HD + 1]
        zero = jnp.zeros_like(v)
        stacked = jnp.concatenate([jnp.where(even_h, v, zero), jnp.where(even_h, zero, v)], axis=0)
        dp = mm_nt(do16, stacked)
        keys = slice(part * SH, (part + 1) * SH)
        e = jnp.concatenate([e_s[l, b, hp * 2, :, keys], e_s[l, b, hp * 2 + 1, :, keys]], axis=1)
        ds = (e.astype(F32) * (dp - jnp.where(low_lane, d0, d1))).astype(BF16)
        dk = mm(q_t, ds)
        dv = mm(do_t, e)
        dk = jnp.concatenate([dk[:HD, :SH], dk[HD:, SH:]], axis=0) * scale
        dv = jnp.concatenate([dv[:HD, :SH], dv[HD:, SH:]], axis=0)
        wide[kr, pl.ds(pl.multiple_of(D + at, 128), 2 * HD)] = dk.astype(BF16).T
        wide[kr, pl.ds(pl.multiple_of(2 * D + at, 128), 2 * HD)] = dv.astype(BF16).T
        return ds

    def back_queries(l, b, hp, low, high):
        at = pl.multiple_of(hp * 2 * HD, 2 * HD)
        sl = pl.ds(at, 2 * HD)
        kr = pl.ds(pl.multiple_of(b * S, 16), S)
        k = k_s[l, kr, sl]
        zero = jnp.zeros_like(k)
        dq = mm(jnp.concatenate([low[:, :SH], high[0]], axis=1), jnp.where(even_k, k, zero))
        dq += mm(jnp.concatenate([low[:, SH:], high[1]], axis=1), jnp.where(even_k, zero, k))
        wide[pl.ds(pl.multiple_of(b * S, 16), TQ), sl] = (dq * scale).astype(BF16)

    def pairs_loop(body, lo, hi):
        def one(i, carry):
            body(i // (H // 2), i % (H // 2))
            return carry

        lax.fori_loop(lo, hi, one, 0, unroll=True)

    pairs = B * H // 2

    def send(src, dst, sems, l, device):
        return pltpu.make_async_remote_copy(
            src_ref=src,
            dst_ref=dst,
            send_sem=sems.at[l, 0],
            recv_sem=sems.at[l, 1],
            device_id=device,
            device_id_type=MESH,
        )

    def all_of(slots, l, count, sems):
        view = slots.at[l, 0:count]
        return send(view, view, sems, l, {"mlp": other})

    mine_b = core * G + g

    def reduce_start(l, grad):
        rows = jnp.concatenate([grad, jnp.zeros((G * PB - grad.shape[0], D), F32)], axis=0)
        for j in range(NJ):
            for k in range(G):
                block = rows[k * PB : (k + 1) * PB, 128 * j : 128 * (j + 1)]
                part_h[l, j // HJ * G + k, j % HJ] = block.astype(BF16)
        for k, c in around:
            to = lax.rem(core + c, 2) * G + member(k)
            send(
                part_h.at[l, to], slot_b.at[l, mine_b], sem_b, l, neighbour(k, c)
            ).start()
        slot_b[l, mine_b] = part_h[l, mine_b]

    def reduce_group(l):
        all_of(slot_b, l, 2 * G - 1, sem_b).wait_recv()
        total = slot_b[l, 0].astype(F32)
        for i in range(1, 2 * G):
            total = total + slot_b[l, i].astype(F32)
        slot_c[l, r] = total.astype(BF16)

        def go(k, carry):
            peer = {"dp": rank(k) * G + g}
            send(slot_c.at[l, r], slot_c.at[l, r], sem_c, l, peer).start()
            return carry

        lax.fori_loop(1, R, go, 0, unroll=R <= 4)
        all_of(part_h, l, 2 * G - 1, sem_b).wait_send()

    def square_of(block):
        block = block.astype(F32)
        total = jnp.sum(jnp.sum(block * block, axis=0), axis=(0, 1), keepdims=True)
        return jnp.broadcast_to(total, (8, 128))

    def reduce_ranks(l):
        if R > 1:
            all_of(slot_c, l, R - 1, sem_c).wait_recv()

        def add(k, total):
            return total + slot_c[l, k].astype(F32)

        total = lax.fori_loop(0, R, add, jnp.zeros((HJ, PB, 128), F32), unroll=R <= 4)
        fin[l, g] = total.astype(BF16)
        for k in range(1, G):
            peer = {"dp": r * G + member(k)}
            send(fin.at[l, g], fin.at[l, g], sem_d, l, peer).start()
        sq_out[l] = square_of(fin[l, g])
        for k in range(G):
            send(sq_out.at[l], sq_in.at[l, g], sem_e, l, neighbour(k, 1)).start()
        if R > 1:
            all_of(slot_c, l, R - 1, sem_c).wait_send()

    def reduce_end(l):
        all_of(fin, l, G - 1, sem_d).wait()
        all_of(sq_in, l, G, sem_e).wait()

    def mlp_chunk(l, part, j, last_):
        cols = slice(j * C, (j + 1) * C)
        at = slice((part * (FH // C) + j) * C, (part * (FH // C) + j + 1) * C)
        pre = mm(x16[...], w_up[l, part, :, cols]) + ub[part, pl.ds(l, 1), cols]
        cdf = 0.5 + 0.5 * lax.erf(pre * 0.7071067811865476)
        if last_ != "output":
            bell = jnp.exp2(pre * pre * (-0.5 * LOG2E)) * 0.3989422804014327
            gp_s[l, :, at] = (cdf + pre * bell).astype(BF16)
        if last_ != "slope":
            add = mm((pre * cdf).astype(BF16), w_dn[l, part, cols, :])
            if part == 0 and j == 0:
                acc[...] = add
            else:
                acc[...] += add

    chunks = [(part, j) for part in range(2) for j in range(FH // C)]

    def forward(l, carry):
        for b in range(B):
            for j in range(NJ):
                seq[b, TK : TK + PN, columns(j)] = prom_v[j, pl.ds(l, PN, stride=L), :]
        gain, shift = norms[l, 0:1, :], norms[l, 1:2, :]
        for b in range(B):
            xh, inv = norm_rows(seq[b])
            at = slice(b * S, (b + 1) * S)
            xh1[l, at, :] = xh.astype(BF16)
            inv_s[l, at, 0:1] = inv
            wide[at, 0:D] = (xh * gain + shift).astype(BF16)
        copy_weight(l, 0).wait()

        @pl.when(l == 0)
        def _():
            copy_small(2).start()
            for i in range(1, 4):
                copy_weight(0, i).start()

        lhs = jnp.concatenate([wide[b * S : b * S + TQ, 0:D] for b in range(B)], axis=0)
        q_s[l] = (mm(lhs, w_qkv[l, :, 0:D]) + bias[l, 0:1, :]).astype(BF16)
        k_s[l] = mm(wide[:, 0:D], w_qkv[l, :, D : 2 * D]).astype(BF16)
        v_s[l] = (mm(wide[:, 0:D], w_qkv[l, :, 2 * D : 3 * D]) + bias[l, 1:2, :]).astype(BF16)
        attend_forward(l)
        copy_weight(l, 1).wait()

        @pl.when(l == 0)
        def _():
            for later in range(1, L):
                for i in range(2):
                    push_weight(later, i).start()
                for i in range(4):
                    copy_weight(later, i).start()
            for j in range(NJ):
                copy_cot(j).start()
            for j in range(HJ):
                copy_moment(0, j).start()
                copy_moment(1, j).start()

        branch = mm(o_s[l], w_out[l]) + bias[l, 2:3, :]
        for b in range(B):
            hid[b * TQ : (b + 1) * TQ, :] = seq[b, 0:TQ, :] + branch[b * TQ : (b + 1) * TQ]
        gain2, shift2 = norms[l, 2:3, :], norms[l, 3:4, :]
        xh, inv = norm_rows(hid[...])
        xh2[l] = xh.astype(BF16)
        inv_s[l, 0 : B * TQ, 1:2] = inv
        x16[...] = (xh * gain2 + shift2).astype(BF16)

        @pl.when(l == 0)
        def _():
            copy_small(2).wait()
            push_ub().wait()

        copy_weight(l, 2).wait()
        copy_weight(l, 3).wait()

        @pl.when(l < L - 1)
        def _():
            for part, j in chunks:
                if part == 1 and j == 0:
                    push_weight(l, 0).wait()
                    push_weight(l, 1).wait()
                mlp_chunk(l, part, j, "both")
            for b in range(B):
                at = slice(b * TQ, (b + 1) * TQ)
                seq[b, 0:TQ, :] = hid[at, :] + acc[at, :] + bias[l, 3:4, :]

        return carry

    lax.fori_loop(0, L, forward, 0)
    for part, j in chunks:
        if part == 1 and j == 0:
            push_weight(L - 1, 0).wait()
            push_weight(L - 1, 1).wait()
        mlp_chunk(L - 1, part, j, "slope")
    for b in range(B):
        seq[b, 0:TQ, :] = hid[b * TQ : (b + 1) * TQ, :] + bias[L - 1, 3:4, :]

    def activations_out():
        for b in range(B):
            seq[b, 0:TQ, :] += acc[b * TQ : (b + 1) * TQ, :]
            for j in range(NJ):
                stage_v[j, pl.ds(b, T, stride=B), :] = seq[b, 0:T, 128 * j : 128 * (j + 1)]
        for j in range(NJ):
            tok_v[j] = stage_v[j].astype(BF16)

    for j in range(NJ):
        copy_cot(j).wait()
    for b in range(B):
        hid[b * TQ + TK - 8 : (b + 1) * TQ, :] = jnp.zeros((TQ - TK + 8, D), F32)

    def store_cot(b, cols, rows):
        hid[b * TQ : b * TQ + T, cols] = rows

    spread(cot_v, store_cot)

    def backward(step, carry):
        l = L - 1 - step
        above = l + 1

        def sum_above(phase):
            pl.when(step > 0)(lambda: phase(above))

        x16[...] = hid[...].astype(BF16)
        for part in range(2):
            for j in range(FH // C):
                cols = slice(j * C, (j + 1) * C)
                at = slice((part * (FH // C) + j) * C, (part * (FH // C) + j + 1) * C)
                ga = mm_nt(x16[...], w_dn[l, part, cols, :])
                gpre = (gp_s[l, :, at].astype(F32) * ga).astype(BF16)
                add = mm_nt(gpre, w_up[l, part, :, cols])
                if part == 0 and j == 0:
                    acc[...] = add
                else:
                    acc[...] += add
            if part == 0:
                sum_above(reduce_group)
        gain2 = norms[l, 2:3, :]

        new = hid[...] + ln_back(
            acc[...], xh2[l].astype(F32), inv_s[l, 0 : B * TQ, 1:2], gain2
        )
        hid[...] = new
        x16[...] = new.astype(BF16)
        x16[...] = mm_nt(x16[...], w_out[l]).astype(BF16)
        gain = norms[l, 0:1, :]

        def high_keys(b, hp):
            ds = back_half(l, b, hp, 1, True)
            e_s[l, b, hp * 2, :, SH:] = ds[:, :SH]
            e_s[l, b, hp * 2 + 1, :, SH:] = ds[:, SH:]

        def low_keys(b, hp):
            ds = back_half(l, b, hp, 0, False)
            back_queries(
                l, b, hp, ds, (e_s[l, b, hp * 2, :, SH:], e_s[l, b, hp * 2 + 1, :, SH:])
            )

        def prompt_gradient():
            base = TK // 16 * 16
            lhs = jnp.concatenate(
                [wide[b * S + base : (b + 1) * S, D : 3 * D] for b in range(B)], axis=0
            )
            full = mm_nt(lhs, w_qkv[l, :, D : 3 * D])
            n = S - base
            dprom = full[TK - base : n]
            for b in range(1, B):
                dprom = dprom + full[b * n + TK - base : (b + 1) * n]
            xh_p = xh1[l, base:S, :].astype(F32)[TK - base :]
            return ln_back(dprom, xh_p, inv_s[l, TK:S, 0:1], gain)

        pairs_loop(high_keys, 0, pairs)
        sum_above(reduce_ranks)
        reduce_start(l, prompt_gradient())
        pairs_loop(low_keys, 0, pairs)
        sum_above(reduce_end)
        lhs = jnp.concatenate([wide[b * S : b * S + TQ, :] for b in range(B)], axis=0)
        acc[...] = mm_nt(lhs, w_qkv[l])
        pl.when(l == 0)(lambda: reduce_group(l))
        for b in range(B):
            at = slice(b * TQ, b * TQ + TK)
            dx = ln_back(
                acc[at, :],
                xh1[l, b * S : b * S + TQ, :].astype(F32)[:TK],
                inv_s[l, b * S : b * S + TK, 0:1],
                gain,
            )
            hid[at, :] = hid[at, :] + dx
        return carry

    lax.fori_loop(0, L, backward, 0)
    x16[...] = (xh2[L - 1].astype(F32) * norms[L - 1, 2:3, :] + norms[L - 1, 3:4, :]).astype(BF16)
    for i, (part, j) in enumerate(chunks):
        if i == len(chunks) - 1:
            reduce_ranks(0)
        mlp_chunk(L - 1, part, j, "output")
    activations_out()
    for j in range(NJ):
        for b in range(B):
            stage_v[j, pl.ds(b, T, stride=B), :] = hid[
                b * TQ : b * TQ + T, 128 * j : 128 * (j + 1)
            ]
    reduce_end(0)

    grad_v = grad_nat.reshape(HJ, PN * L, 128)
    for l in range(L):
        for k in range(G):
            rows = min(PB, PN - k * PB)
            for j in range(HJ):
                grad_v[j, pl.ds(k * PB * L + l, rows, stride=L), :] = fin[l, k, j].astype(F32)[:rows]
    n = PN * L
    own, theirs = jnp.zeros((8, 128), F32), jnp.zeros((8, 128), F32)
    for l in range(L):
        for k in range(G):
            own += square_of(fin[l, k])
            theirs += sq_in[l, k]
    squares = own + theirs
    grad_norm = jnp.sqrt(squares)
    norm_s[...] = grad_norm[0:1, 0:1]
    factor = jnp.minimum(1.0, clip_limit / (grad_norm[0:1, :] + 1e-06))
    fix_first = 1.0 - beta_one**STEP
    fix_second = 1.0 - beta_two**STEP
    for j in range(HJ):
        copy_moment(0, j).wait()
        copy_moment(1, j).wait()
        first_v = first_nat.reshape(HJ, n, 128)
        second_v = second_nat.reshape(HJ, n, 128)
        prompt_v = prompt_nat.reshape(HJ, n, 128)
        clipped = grad_v[j, 0:n, :] * factor
        new_first = beta_one * first_v[j, 0:n, :] + (1.0 - beta_one) * clipped
        new_second = beta_two * second_v[j, 0:n, :] + (1.0 - beta_two) * clipped * clipped
        first_v[j, 0:n, :] = new_first
        second_v[j, 0:n, :] = new_second
        old = prom_v[core * HJ + j]
        prompt_v[j] = old - learn_rate * (
            new_first / fix_first / (jnp.sqrt(new_second / fix_second) + adam_eps)
            + weight_decay * old
        )


def hand_on_kernel(*refs):
    n = (len(refs) - 1) // 2
    sources, targets, sem = refs[:n], refs[n : 2 * n], refs[2 * n]
    copies = []
    for src, dst in zip(sources, targets):
        if len(src.shape) == 2:
            copies.append(pltpu.make_async_copy(src, dst, sem.at[len(copies)]))
        else:
            for j in range(src.shape[0]):
                view = dst.at[:, :, 128 * j : 128 * (j + 1)]
                copies.append(pltpu.make_async_copy(src.at[j], view, sem.at[len(copies)]))
    for copy in copies:
        copy.start()
    for copy in copies:
        copy.wait()


def hand_on(arrays):
    def whole(a):
        shape = a.shape if len(a.shape) == 2 else a.shape[1:3] + (a.shape[0] * a.shape[3],)
        return jax.ShapeDtypeStruct(shape, a.dtype)

    count = sum(1 if len(a.shape) == 2 else a.shape[0] for a in arrays)
    return pl.pallas_call(
        hand_on_kernel,
        out_shape=tuple(whole(a) for a in arrays),
        in_specs=[pl.BlockSpec(memory_space=VMEM)] * len(arrays),
        out_specs=(pl.BlockSpec(memory_space=pl.ANY),) * len(arrays),
        scratch_shapes=[DMA((count,))],
        compiler_params=pltpu.CompilerParams(vmem_limit_bytes=2**20),
    )(*arrays)


def native(x):
    return x.transpose(1, 0, 2)


def local(
    ndp, tokens, cotangent, prompts, first_moment, second_moment, norm_params, bias_rows,
    qkv_weight, out_weight, up_weight, up_bias, down_weight,
):
    B, T, D = tokens.shape
    L, PN, _ = prompts.shape
    FH = down_weight.shape[1]
    TK = up_to(T, 8)
    S = up_to(TK + up_to(PN, 8), 128)
    TQ = up_to(T, 16)
    G = 4
    R = ndp // G
    NJ, HJ, PB = D // 128, D // 256, 16
    dims = (B, T, D, L, PN, TK, S, TQ, FH, G, R)
    H = HEADS
    n_local = 2 * NJ + 3 * HJ + 3
    scratch = [
        VMEM((NJ, T, B, 128), BF16),
        VMEM((NJ, PN, L, 128), F32),
        VMEM((L, 4, D), F32),
        VMEM((L, 4, D), F32),
        VMEM((L, D, 3 * D), BF16),
        VMEM((L, D, D), BF16),
        VMEM((L, 2, D, FH), BF16),
        VMEM((2, L, FH), F32),
        VMEM((L, 2, FH, D), BF16),
        VMEM((B, S, D), F32),
        VMEM((B * TQ, D), F32),
        VMEM((B * TQ, D), F32),
        VMEM((B * S, 3 * D), BF16),
        VMEM((B * TQ, D), BF16),
        VMEM((L, B * S, D), BF16),
        VMEM((L, B * TQ, D), BF16),
        VMEM((L, B * S, 2), F32),
        VMEM((L, B * TQ, D), BF16),
        VMEM((L, B * S, D), BF16),
        VMEM((L, B * S, D), BF16),
        VMEM((L, B, H, TQ, S), BF16),
        VMEM((L, B * TQ, D), BF16),
        VMEM((L, B * TQ, D), BF16),
        VMEM((L, B * TQ, 2 * FH), BF16),
        VMEM((L, 2 * G, HJ, PB, 128), BF16),
        VMEM((L, 2 * G, HJ, PB, 128), BF16),
        VMEM((L, R, HJ, PB, 128), BF16),
        VMEM((L, G, HJ, PB, 128), BF16),
        VMEM((L, 8, 128), F32),
        VMEM((L, G, 8, 128), F32),
        DMA((n_local,)),
        DMA((L, 4)),
        DMA((2, HJ + 1)),
        DMA((L, 2, 2)),
        DMA((L, 2)),
        DMA((L, 2)),
        DMA((L, 2)),
        DMA((L, 2)),
    ]
    any_spec = pl.BlockSpec(memory_space=pl.ANY)
    small = jax.ShapeDtypeStruct((HJ, PN, L, 128), F32)
    small_v = VMEM((HJ, PN, L, 128), F32)
    results = pl.pallas_call(
        functools.partial(main_kernel, dims),
        out_shape=(
            VMEM((NJ, T, B, 128), BF16),
            VMEM((NJ, T, B, 128), F32),
            small_v,
            VMEM((1, 1), F32),
            small_v,
            small_v,
            small_v,
        ),
        in_specs=[any_spec] * 12,
        scratch_shapes=scratch,
        compiler_params=pltpu.CompilerParams(
            collective_id=0, has_side_effects=True, vmem_limit_bytes=61 * 2**20
        ),
    )(
        native(tokens), native(cotangent), native(prompts), native(first_moment),
        native(second_moment), norm_params, bias_rows, qkv_weight, out_weight,
        up_weight, up_bias, down_weight,
    )
    act, igrad, grad, norm, new_first, new_second, new_prompts = hand_on(results)
    return (
        native(act), native(igrad), native(grad), norm.reshape(()),
        native(new_first), native(new_second), native(new_prompts),
    )


def solution(mesh):
    ndp = mesh.shape["dp"]
    return jax.shard_map(
        functools.partial(local, ndp),
        mesh=mesh,
        in_specs=(
            P(("dp", "mlp"), None, None),
            P(("dp", "mlp"), None, None),
            P(None, None, "mlp"),
            P(None, None, "mlp"),
            P(None, None, "mlp"),
            P(),
            P(),
            P(),
            P(),
            P(None, None, "mlp"),
            P(None, "mlp"),
            P(None, "mlp", None),
        ),
        out_specs=(
            P(("dp", "mlp"), None, None),
            P(("dp", "mlp"), None, None),
            P(None, None, "mlp"),
            P(),
            P(None, None, "mlp"),
            P(None, None, "mlp"),
            P(None, None, "mlp"),
        ),
        check_vma=False,
    )
```

profile of v0, /device:TPU:0, one launch (start us, length us, event | category | flops | bytes accessed | tf_op | source)
XLA Modules:
  0.0 72.9 jit_solution(658884427672108768)
XLA Ops:
  0.6 69.8 %shard_map.171 = (bf16[6,197,2,128]{3,2,1,0:T(2,128)(2,1)S(1)}, f32[6,197,2,128]{3,2,1,0:T(2,128)S(1)}, f32[3,50,2,128]{3,2,1,0:T(2,128)S(1)}, f32[1,1]{1,0:T(1,...) custom-call(bf16[197,2,768]{2,1,0:T(2,128)(2,1)} %bitcast.12, ...), custom_call_target="tpu_custom_call" | custom-call | tf_op jit(solution)/shard_map/pallas_call | solution.py:760
  70.5 2.3 %shard_map.172 = (bf16[197,2,768]{2,1,0:T(2,128)(2,1)}, f32[197,2,768]{2,1,0:T(2,128)}, f32[50,2,384]{2,1,0:T(2,128)}, f32[1,1]{1,0:T(1,128)}, f32[50,2,384]{2,1...) custom-call(bf16[6,197,2,128]{3,2,1,0:T(2,128)(2,1)S(1)} %get-tuple-element.21.refs_0_, ...), custom_call_target="tpu_custom_call" | custom-call | tf_op jit(solution)/shard_map/pallas_call | solution.py:687
where the time goes:
time: 73.1 us; the launch traced here: 72.9 us
  Pallas kernels  72.1 us (99%)
  between operations  0.83 us (1%)
    pallas_call x1, Pallas kernels, local(): pl.pallas_call(functools.partial(main_kernel, dims), out_shape=(VMEM((NJ,...  69.8 us
    pallas_call x1, Pallas kernels, hand_on(): pl.pallas_call(hand_on_kernel, out_shape=tuple((whole(a) for a in arrays)...  2.26 us

commit v1 on v0

--- a/solution.py
+++ b/solution.py
@@ -109,7 +109,7 @@
     sem_d,
     sem_e,
 ):
-    B, T, D, L, PN, TK, S, TQ, FH, G, R = dims
+    B, T, D, L, PN, TK, PP, S, TQ, FH, G, R = dims
     H = HEADS
     HD = D // H
     C = 768
@@ -152,18 +152,20 @@
         return pltpu.make_async_copy(src, dst, local_sem.at[i])
 
     def copy_tok(j):
-        return local(j, tok_hbm.at[:, :, columns(j)], tok_nat.at[j])
+        return local(j, tok_hbm.at[:, :, columns(j)], tok_nat.at[j, 0:T])
 
     def copy_cot(j):
-        return local(NJ + j, cot_hbm.at[:, :, columns(j)], cot_nat.at[j])
+        return local(NJ + j, cot_hbm.at[:, :, columns(j)], cot_nat.at[j, 0:T])
 
     def copy_prom(j):
-        return local(2 * NJ + j, prompts_hbm.at[:, :, columns(j)], prom_nat.at[core * HJ + j])
+        return local(
+            2 * NJ + j, prompts_hbm.at[:, :, columns(j)], prom_nat.at[core * HJ + j, 0:PN]
+        )
 
     def copy_moment(i, j):
         src = (first_hbm, second_hbm)[i]
         return local(
-            2 * NJ + (i + 1) * HJ + j, src.at[:, :, columns(j)], (first_nat, second_nat)[i].at[j]
+            2 * NJ + (i + 1) * HJ + j, src.at[:, :, columns(j)], (first_nat, second_nat)[i].at[j, 0:PN]
         )
 
     def copy_small(i):
@@ -192,7 +194,7 @@
     def push_prom(j):
         return push(
             prompts_hbm.at[:, :, columns(j)],
-            prom_nat.at[core * HJ + j],
+            prom_nat.at[core * HJ + j, 0:PN],
             push_sem.at[0, j],
             push_sem.at[1, j],
         )
@@ -218,10 +220,10 @@
     push_weight(0, 0).start()
     push_weight(0, 1).start()
 
-    tok_v = tok_nat.reshape(NJ, T * B, 128)
-    cot_v = cot_nat.reshape(NJ, T * B, 128)
-    stage_v = stage_nat.reshape(NJ, T * B, 128)
-    prom_v = prom_nat.reshape(NJ, PN * L, 128)
+    tok_v = tok_nat.reshape(NJ, TK * B, 128)
+    cot_v = cot_nat.reshape(NJ, TK * B, 128)
+    stage_v = stage_nat.reshape(NJ, TK * B, 128)
+    prom_v = prom_nat.reshape(NJ, PP * L, 128)
 
     lane = lax.broadcasted_iota(jnp.int32, (1, S), 1)
     valid = (lane < T) | ((lane >= TK) & (lane < TK + PN))
@@ -235,7 +237,7 @@
 
     def spread(src_v, store):
         for j in range(NJ):
-            stage_v[j] = src_v[j].astype(F32)
+            stage_v[j, 0 : T * B] = src_v[j, 0 : T * B].astype(F32)
         for b in range(B):
             for j in range(NJ):
                 store(b, slice(128 * j, 128 * (j + 1)), stage_v[j, pl.ds(b, T, stride=B), :])
@@ -441,7 +443,7 @@
 
     chunks = [(part, j) for part in range(2) for j in range(FH // C)]
 
-    def forward(l, carry):
+    def norm_one(l):
         for b in range(B):
             for j in range(NJ):
                 seq[b, TK : TK + PN, columns(j)] = prom_v[j, pl.ds(l, PN, stride=L), :]
@@ -452,20 +454,34 @@
             xh1[l, at, :] = xh.astype(BF16)
             inv_s[l, at, 0:1] = inv
             wide[at, 0:D] = (xh * gain + shift).astype(BF16)
-        copy_weight(l, 0).wait()
-
-        @pl.when(l == 0)
-        def _():
-            copy_small(2).start()
-            for i in range(1, 4):
-                copy_weight(0, i).start()
-
+
+    def attend(l):
         lhs = jnp.concatenate([wide[b * S : b * S + TQ, 0:D] for b in range(B)], axis=0)
         q_s[l] = (mm(lhs, w_qkv[l, :, 0:D]) + bias[l, 0:1, :]).astype(BF16)
         k_s[l] = mm(wide[:, 0:D], w_qkv[l, :, D : 2 * D]).astype(BF16)
         v_s[l] = (mm(wide[:, 0:D], w_qkv[l, :, 2 * D : 3 * D]) + bias[l, 1:2, :]).astype(BF16)
         attend_forward(l)
-        copy_weight(l, 1).wait()
+
+    def norm_two(l):
+        branch = mm(o_s[l], w_out[l]) + bias[l, 2:3, :]
+        for b in range(B):
+            hid[b * TQ : (b + 1) * TQ, :] = seq[b, 0:TQ, :] + branch[b * TQ : (b + 1) * TQ]
+        gain2, shift2 = norms[l, 2:3, :], norms[l, 3:4, :]
+        xh, inv = norm_rows(hid[...])
+        xh2[l] = xh.astype(BF16)
+        inv_s[l, 0 : B * TQ, 1:2] = inv
+        x16[...] = (xh * gain2 + shift2).astype(BF16)
+
+    norm_one(0)
+    copy_weight(0, 0).wait()
+    copy_small(2).start()
+    for i in range(1, 4):
+        copy_weight(0, i).start()
+
+    def forward(l, carry):
+        attend(l)
+        for i in range(1, 4):
+            copy_weight(l, i).wait()
 
         @pl.when(l == 0)
         def _():
@@ -479,26 +495,12 @@
             for j in range(HJ):
                 copy_moment(0, j).start()
                 copy_moment(1, j).start()
-
-        branch = mm(o_s[l], w_out[l]) + bias[l, 2:3, :]
-        for b in range(B):
-            hid[b * TQ : (b + 1) * TQ, :] = seq[b, 0:TQ, :] + branch[b * TQ : (b + 1) * TQ]
-        gain2, shift2 = norms[l, 2:3, :], norms[l, 3:4, :]
-        xh, inv = norm_rows(hid[...])
-        xh2[l] = xh.astype(BF16)
-        inv_s[l, 0 : B * TQ, 1:2] = inv
-        x16[...] = (xh * gain2 + shift2).astype(BF16)
-
-        @pl.when(l == 0)
-        def _():
             copy_small(2).wait()
             push_ub().wait()
 
-        copy_weight(l, 2).wait()
-        copy_weight(l, 3).wait()
-
         @pl.when(l < L - 1)
         def _():
+            norm_two(l)
             for part, j in chunks:
                 if part == 1 and j == 0:
                     push_weight(l, 0).wait()
@@ -507,14 +509,18 @@
             for b in range(B):
                 at = slice(b * TQ, (b + 1) * TQ)
                 seq[b, 0:TQ, :] = hid[at, :] + acc[at, :] + bias[l, 3:4, :]
+            norm_one(l + 1)
+            copy_weight(l + 1, 0).wait()
 
         return carry
 
     lax.fori_loop(0, L, forward, 0)
+    push_weight(L - 1, 0).wait()
+    push_weight(L - 1, 1).wait()
+    for j in range(NJ):
+        copy_cot(j).wait()
+    norm_two(L - 1)
     for part, j in chunks:
-        if part == 1 and j == 0:
-            push_weight(L - 1, 0).wait()
-            push_weight(L - 1, 1).wait()
         mlp_chunk(L - 1, part, j, "slope")
     for b in range(B):
         seq[b, 0:TQ, :] = hid[b * TQ : (b + 1) * TQ, :] + bias[L - 1, 3:4, :]
@@ -525,10 +531,8 @@
             for j in range(NJ):
                 stage_v[j, pl.ds(b, T, stride=B), :] = seq[b, 0:T, 128 * j : 128 * (j + 1)]
         for j in range(NJ):
-            tok_v[j] = stage_v[j].astype(BF16)
-
-    for j in range(NJ):
-        copy_cot(j).wait()
+            tok_v[j, 0 : T * B] = stage_v[j, 0 : T * B].astype(BF16)
+
     for b in range(B):
         hid[b * TQ + TK - 8 : (b + 1) * TQ, :] = jnp.zeros((TQ - TK + 8, D), F32)
 
@@ -545,6 +549,7 @@
             pl.when(step > 0)(lambda: phase(above))
 
         x16[...] = hid[...].astype(BF16)
+        sum_above(reduce_group)
         for part in range(2):
             for j in range(FH // C):
                 cols = slice(j * C, (j + 1) * C)
@@ -556,8 +561,6 @@
                     acc[...] = add
                 else:
                     acc[...] += add
-            if part == 0:
-                sum_above(reduce_group)
         gain2 = norms[l, 2:3, :]
 
         new = hid[...] + ln_back(
@@ -593,13 +596,13 @@
             return ln_back(dprom, xh_p, inv_s[l, TK:S, 0:1], gain)
 
         pairs_loop(high_keys, 0, pairs)
+        reduce_start(l, prompt_gradient())
         sum_above(reduce_ranks)
-        reduce_start(l, prompt_gradient())
         pairs_loop(low_keys, 0, pairs)
-        sum_above(reduce_end)
         lhs = jnp.concatenate([wide[b * S : b * S + TQ, :] for b in range(B)], axis=0)
         acc[...] = mm_nt(lhs, w_qkv[l])
         pl.when(l == 0)(lambda: reduce_group(l))
+        sum_above(reduce_end)
         for b in range(B):
             at = slice(b * TQ, b * TQ + TK)
             dx = ln_back(
@@ -625,7 +628,7 @@
             ]
     reduce_end(0)
 
-    grad_v = grad_nat.reshape(HJ, PN * L, 128)
+    grad_v = grad_nat.reshape(HJ, PP * L, 128)
     for l in range(L):
         for k in range(G):
             rows = min(PB, PN - k * PB)
@@ -646,16 +649,16 @@
     for j in range(HJ):
         copy_moment(0, j).wait()
         copy_moment(1, j).wait()
-        first_v = first_nat.reshape(HJ, n, 128)
-        second_v = second_nat.reshape(HJ, n, 128)
-        prompt_v = prompt_nat.reshape(HJ, n, 128)
+        first_v = first_nat.reshape(HJ, PP * L, 128)
+        second_v = second_nat.reshape(HJ, PP * L, 128)
+        prompt_v = prompt_nat.reshape(HJ, PP * L, 128)
         clipped = grad_v[j, 0:n, :] * factor
         new_first = beta_one * first_v[j, 0:n, :] + (1.0 - beta_one) * clipped
         new_second = beta_two * second_v[j, 0:n, :] + (1.0 - beta_two) * clipped * clipped
         first_v[j, 0:n, :] = new_first
         second_v[j, 0:n, :] = new_second
-        old = prom_v[core * HJ + j]
-        prompt_v[j] = old - learn_rate * (
+        old = prom_v[core * HJ + j, 0:n, :]
+        prompt_v[j, 0:n, :] = old - learn_rate * (
             new_first / fix_first / (jnp.sqrt(new_second / fix_second) + adam_eps)
             + weight_decay * old
         )
@@ -669,27 +672,30 @@
         if len(src.shape) == 2:
             copies.append(pltpu.make_async_copy(src, dst, sem.at[len(copies)]))
         else:
+            rows = dst.shape[0]
             for j in range(src.shape[0]):
                 view = dst.at[:, :, 128 * j : 128 * (j + 1)]
-                copies.append(pltpu.make_async_copy(src.at[j], view, sem.at[len(copies)]))
+                copies.append(
+                    pltpu.make_async_copy(src.at[j, 0:rows], view, sem.at[len(copies)])
+                )
     for copy in copies:
         copy.start()
     for copy in copies:
         copy.wait()
 
 
-def hand_on(arrays):
-    def whole(a):
-        shape = a.shape if len(a.shape) == 2 else a.shape[1:3] + (a.shape[0] * a.shape[3],)
+def hand_on(arrays, counts):
+    def whole(a, rows):
+        shape = a.shape if len(a.shape) == 2 else (rows, a.shape[2], a.shape[0] * a.shape[3])
         return jax.ShapeDtypeStruct(shape, a.dtype)
 
-    count = sum(1 if len(a.shape) == 2 else a.shape[0] for a in arrays)
+    copies = sum(1 if len(a.shape) == 2 else a.shape[0] for a in arrays)
     return pl.pallas_call(
         hand_on_kernel,
-        out_shape=tuple(whole(a) for a in arrays),
+        out_shape=tuple(whole(a, rows) for a, rows in zip(arrays, counts)),
         in_specs=[pl.BlockSpec(memory_space=VMEM)] * len(arrays),
         out_specs=(pl.BlockSpec(memory_space=pl.ANY),) * len(arrays),
-        scratch_shapes=[DMA((count,))],
+        scratch_shapes=[DMA((copies,))],
         compiler_params=pltpu.CompilerParams(vmem_limit_bytes=2**20),
     )(*arrays)
 
@@ -706,17 +712,18 @@
     L, PN, _ = prompts.shape
     FH = down_weight.shape[1]
     TK = up_to(T, 8)
-    S = up_to(TK + up_to(PN, 8), 128)
+    PP = up_to(PN, 8)
+    S = up_to(TK + PP, 128)
     TQ = up_to(T, 16)
     G = 4
     R = ndp // G
     NJ, HJ, PB = D // 128, D // 256, 16
-    dims = (B, T, D, L, PN, TK, S, TQ, FH, G, R)
+    dims = (B, T, D, L, PN, TK, PP, S, TQ, FH, G, R)
     H = HEADS
     n_local = 2 * NJ + 3 * HJ + 3
     scratch = [
-        VMEM((NJ, T, B, 128), BF16),
-        VMEM((NJ, PN, L, 128), F32),
+        VMEM((NJ, TK, B, 128), BF16),
+        VMEM((NJ, PP, L, 128), F32),
         VMEM((L, 4, D), F32),
         VMEM((L, 4, D), F32),
         VMEM((L, D, 3 * D), BF16),
@@ -755,18 +762,17 @@
         DMA((L, 2)),
     ]
     any_spec = pl.BlockSpec(memory_space=pl.ANY)
-    small = jax.ShapeDtypeStruct((HJ, PN, L, 128), F32)
-    small_v = VMEM((HJ, PN, L, 128), F32)
+    small = VMEM((HJ, PP, L, 128), F32)
     results = pl.pallas_call(
         functools.partial(main_kernel, dims),
         out_shape=(
-            VMEM((NJ, T, B, 128), BF16),
-            VMEM((NJ, T, B, 128), F32),
-            small_v,
+            VMEM((NJ, TK, B, 128), BF16),
+            VMEM((NJ, TK, B, 128), F32),
+            small,
             VMEM((1, 1), F32),
-            small_v,
-            small_v,
-            small_v,
+            small,
+            small,
+            small,
         ),
         in_specs=[any_spec] * 12,
         scratch_shapes=scratch,
@@ -778,7 +784,9 @@
         native(second_moment), norm_params, bias_rows, qkv_weight, out_weight,
         up_weight, up_bias, down_weight,
     )
-    act, igrad, grad, norm, new_first, new_second, new_prompts = hand_on(results)
+    act, igrad, grad, norm, new_first, new_second, new_prompts = hand_on(
+        results, (T, T, PN, 1, PN, PN, PN)
+    )
     return (
         native(act), native(igrad), native(grad), norm.reshape(()),
         native(new_first), native(new_second), native(new_prompts),

time: 73.1 us -> 70.7 us (0.967)
  Pallas kernels: 72.1 us -> 69.7 us
    pallas_call x1, Pallas kernels: 69.8 us -> 67.5 us  [local(): pl.pallas_call(functools.partial(main_kernel, dims), out_shape=(VMEM((NJ,...]
where the time goes in v1:
time: 70.7 us; the launch traced here: 70.6 us
  Pallas kernels  69.7 us (99%)
  between operations  0.83 us (1%)
    pallas_call x1, Pallas kernels, local(): pl.pallas_call(functools.partial(main_kernel, dims), out_shape=(VMEM((NJ,...  67.5 us
    pallas_call x1, Pallas kernels, hand_on(): pl.pallas_call(hand_on_kernel, out_shape=tuple((whole(a, rows) for a, row...  2.26 us

profile of v1, /device:TPU:0, one launch (start us, length us, event | category | flops | bytes accessed | tf_op | source)
XLA Modules:
  0.0 70.6 jit_solution(17475124143234449227)
XLA Ops:
  0.6 67.5 %shard_map.171 = (bf16[6,200,2,128]{3,2,1,0:T(2,128)(2,1)S(1)}, f32[6,200,2,128]{3,2,1,0:T(2,128)S(1)}, f32[3,56,2,128]{3,2,1,0:T(2,128)S(1)}, f32[1,1]{1,0:T(1,...) custom-call(bf16[197,2,768]{2,1,0:T(2,128)(2,1)} %bitcast.12, ...), custom_call_target="tpu_custom_call" | custom-call | tf_op jit(solution)/shard_map/pallas_call | solution.py:766
  68.1 2.3 %shard_map.172 = (bf16[197,2,768]{2,1,0:T(2,128)(2,1)}, f32[197,2,768]{2,1,0:T(2,128)}, f32[50,2,384]{2,1,0:T(2,128)}, f32[1,1]{1,0:T(1,128)}, f32[50,2,384]{2,1...) custom-call(bf16[6,200,2,128]{3,2,1,0:T(2,128)(2,1)S(1)} %get-tuple-element.21.refs_0_, ...), custom_call_target="tpu_custom_call" | custom-call | tf_op jit(solution)/shard_map/pallas_call | solution.py:693

commit v2 on v1

--- a/solution.py
+++ b/solution.py
@@ -133,18 +133,6 @@
     def neighbour(k, c):
         return {"dp": r * G + member(k), "mlp": lax.rem(core + c, 2)}
 
-    barrier = pltpu.get_barrier_semaphore()
-    for k, c in around:
-        pl.semaphore_signal(barrier, inc=1, device_id=neighbour(k, c), device_id_type=MESH)
-
-    def greet(k, carry):
-        pl.semaphore_signal(
-            barrier, inc=1, device_id={"dp": rank(k) * G + g}, device_id_type=MESH
-        )
-        return carry
-
-    lax.fori_loop(1, R, greet, 0)
-
     def columns(j):
         return slice(128 * j, 128 * (j + 1))
 
@@ -206,13 +194,24 @@
         src, dst = ((up_hbm.at[l], w_up.at[l, 1]), (dn_hbm.at[l], w_dn.at[l, 1]))[i]
         return push(src, dst, push_w_sem.at[l, 0, i], push_w_sem.at[l, 1, i])
 
+    copy_weight(0, 0).start()
+    barrier = pltpu.get_barrier_semaphore()
+    for k, c in around:
+        pl.semaphore_signal(barrier, inc=1, device_id=neighbour(k, c), device_id_type=MESH)
+
+    def greet(k, carry):
+        pl.semaphore_signal(
+            barrier, inc=1, device_id={"dp": rank(k) * G + g}, device_id_type=MESH
+        )
+        return carry
+
+    lax.fori_loop(1, R, greet, 0)
     for j in range(NJ):
         copy_tok(j).start()
     for j in range(HJ):
         copy_prom(j).start()
     copy_small(0).start()
     copy_small(1).start()
-    copy_weight(0, 0).start()
     pl.semaphore_wait(barrier, len(around) + R - 1)
     for j in range(HJ):
         push_prom(j).start()
@@ -270,32 +269,41 @@
         c = jnp.mean(gdy * xh, axis=-1, keepdims=True)
         return inv * (gdy - a - xh * c)
 
+    def scores_at(n):
+        place, n = (acc, n) if n < B * (D // S) else (hid, n - B * (D // S))
+        rows, cols = n // (D // S) * TQ, n % (D // S) * S
+        return place.at[rows : rows + TQ, cols : cols + S]
+
     def attend_forward(l):
-        def pair(i, carry):
-            b = i // (H // 2)
-            hp = i % (H // 2)
-            sl = pl.ds(pl.multiple_of(hp * 2 * HD, 2 * HD), 2 * HD)
+        def image(b, carry):
             qr = pl.ds(pl.multiple_of(b * TQ, 16), TQ)
             kr = pl.ds(pl.multiple_of(b * S, 16), S)
-            q = q_s[l, qr, sl]
-            k = k_s[l, kr, sl]
-            v = v_s[l, kr, sl]
-            sums = []
-            for h in range(2):
-                here = even_k if h == 0 else jnp.logical_not(even_k)
-                s = mm_nt(q, jnp.where(here, k, jnp.zeros_like(k))) + key_bias
-                top = jnp.max(s, axis=1, keepdims=True)
-                e = jnp.exp2((s - top) * (LOG2E * scale)).astype(BF16)
-                e_s[l, b, hp * 2 + h] = e
-                sums.append(mm(e, jnp.where(here, v, jnp.ones_like(v))))
-            top_part = jnp.where(even_q, sums[0], sums[1])
-            total = jnp.where(even_q, sums[1], sums[0])
-            inv = pltpu.roll(1.0 / total, HD, 1)
-            ri_s[l, qr, sl] = inv.astype(BF16)
-            o_s[l, qr, sl] = (top_part * inv).astype(BF16)
+            for hp in range(H // 2):
+                sl = slice(2 * HD * hp, 2 * HD * (hp + 1))
+                q = q_s[l, qr, sl]
+                k = k_s[l, kr, sl]
+                zero = jnp.zeros_like(k)
+                scores_at(2 * hp)[...] = mm_nt(q, jnp.where(even_k, k, zero))
+                scores_at(2 * hp + 1)[...] = mm_nt(q, jnp.where(even_k, zero, k))
+            for hp in range(H // 2):
+                sl = slice(2 * HD * hp, 2 * HD * (hp + 1))
+                v = v_s[l, kr, sl]
+                sums = []
+                for h in range(2):
+                    here = even_k if h == 0 else jnp.logical_not(even_k)
+                    s = scores_at(2 * hp + h)[...] + key_bias
+                    top = jnp.max(s, axis=1, keepdims=True)
+                    e = jnp.exp2((s - top) * (LOG2E * scale)).astype(BF16)
+                    e_s[l, b, hp * 2 + h] = e
+                    sums.append(mm(e, jnp.where(here, v, jnp.ones_like(v))))
+                top_part = jnp.where(even_q, sums[0], sums[1])
+                total = jnp.where(even_q, sums[1], sums[0])
+                inv = pltpu.roll(1.0 / total, HD, 1)
+                ri_s[l, qr, sl] = inv.astype(BF16)
+                o_s[l, qr, sl] = (top_part * inv).astype(BF16)
             return carry
 
-        lax.fori_loop(0, B * H // 2, pair, 0, unroll=6)
+        lax.fori_loop(0, B, image, 0)
 
     def back_half(l, b, hp, part, first):
         at = pl.multiple_of(hp * 2 * HD, 2 * HD)
@@ -401,8 +409,10 @@
 
     def square_of(block):
         block = block.astype(F32)
-        total = jnp.sum(jnp.sum(block * block, axis=0), axis=(0, 1), keepdims=True)
-        return jnp.broadcast_to(total, (8, 128))
+        total = block[0] * block[0]
+        for j in range(1, HJ):
+            total += block[j] * block[j]
+        return total
 
     def reduce_ranks(l):
         if R > 1:
@@ -492,9 +502,6 @@
                     copy_weight(later, i).start()
             for j in range(NJ):
                 copy_cot(j).start()
-            for j in range(HJ):
-                copy_moment(0, j).start()
-                copy_moment(1, j).start()
             copy_small(2).wait()
             push_ub().wait()
 
@@ -548,8 +555,8 @@
         def sum_above(phase):
             pl.when(step > 0)(lambda: phase(above))
 
+        sum_above(reduce_group)
         x16[...] = hid[...].astype(BF16)
-        sum_above(reduce_group)
         for part in range(2):
             for j in range(FH // C):
                 cols = slice(j * C, (j + 1) * C)
@@ -567,8 +574,7 @@
             acc[...], xh2[l].astype(F32), inv_s[l, 0 : B * TQ, 1:2], gain2
         )
         hid[...] = new
-        x16[...] = new.astype(BF16)
-        x16[...] = mm_nt(x16[...], w_out[l]).astype(BF16)
+        x16[...] = mm_nt(new.astype(BF16), w_out[l]).astype(BF16)
         gain = norms[l, 0:1, :]
 
         def high_keys(b, hp):
@@ -615,9 +621,12 @@
         return carry
 
     lax.fori_loop(0, L, backward, 0)
+    for j in range(HJ):
+        copy_moment(0, j).start()
+        copy_moment(1, j).start()
     x16[...] = (xh2[L - 1].astype(F32) * norms[L - 1, 2:3, :] + norms[L - 1, 3:4, :]).astype(BF16)
     for i, (part, j) in enumerate(chunks):
-        if i == len(chunks) - 1:
+        if i == len(chunks) - 2:
             reduce_ranks(0)
         mlp_chunk(L - 1, part, j, "output")
     activations_out()
@@ -635,15 +644,15 @@
             for j in range(HJ):
                 grad_v[j, pl.ds(k * PB * L + l, rows, stride=L), :] = fin[l, k, j].astype(F32)[:rows]
     n = PN * L
-    own, theirs = jnp.zeros((8, 128), F32), jnp.zeros((8, 128), F32)
+    own, theirs = jnp.zeros((PB, 128), F32), jnp.zeros((PB, 128), F32)
     for l in range(L):
         for k in range(G):
             own += square_of(fin[l, k])
             theirs += sq_in[l, k]
-    squares = own + theirs
+    squares = jnp.sum(own + theirs, axis=(0, 1), keepdims=True)
     grad_norm = jnp.sqrt(squares)
-    norm_s[...] = grad_norm[0:1, 0:1]
-    factor = jnp.minimum(1.0, clip_limit / (grad_norm[0:1, :] + 1e-06))
+    norm_s[...] = grad_norm
+    factor = jnp.minimum(1.0, clip_limit / (grad_norm + 1e-06))
     fix_first = 1.0 - beta_one**STEP
     fix_second = 1.0 - beta_two**STEP
     for j in range(HJ):
@@ -750,8 +759,8 @@
         VMEM((L, 2 * G, HJ, PB, 128), BF16),
         VMEM((L, R, HJ, PB, 128), BF16),
         VMEM((L, G, HJ, PB, 128), BF16),
-        VMEM((L, 8, 128), F32),
-        VMEM((L, G, 8, 128), F32),
+        VMEM((L, PB, 128), F32),
+        VMEM((L, G, PB, 128), F32),
         DMA((n_local,)),
         DMA((L, 4)),
         DMA((2, HJ + 1)),

time: 70.7 us -> 68.6 us (0.970)
  Pallas kernels: 69.7 us -> 67.7 us
    pallas_call x1, Pallas kernels: 67.5 us -> 65.4 us  [local(): pl.pallas_call(functools.partial(main_kernel, dims), out_shape=(VMEM((NJ,...]
where the time goes in v2:
time: 68.6 us; the launch traced here: 68.5 us
  Pallas kernels  67.7 us (99%)
  between operations  0.83 us (1%)
    pallas_call x1, Pallas kernels, local(): pl.pallas_call(functools.partial(main_kernel, dims), out_shape=(VMEM((NJ,...  65.4 us
    pallas_call x1, Pallas kernels, hand_on(): pl.pallas_call(hand_on_kernel, out_shape=tuple((whole(a, rows) for a, row...  2.26 us

profile of v2, /device:TPU:0, one launch (start us, length us, event | category | flops | bytes accessed | tf_op | source)
XLA Modules:
  0.0 68.5 jit_solution(13817424663870125278)
XLA Ops:
  0.6 65.4 %shard_map.171 = (bf16[6,200,2,128]{3,2,1,0:T(2,128)(2,1)S(1)}, f32[6,200,2,128]{3,2,1,0:T(2,128)S(1)}, f32[3,56,2,128]{3,2,1,0:T(2,128)S(1)}, f32[1,1]{1,0:T(1,...) custom-call(bf16[197,2,768]{2,1,0:T(2,128)(2,1)} %bitcast.12, ...), custom_call_target="tpu_custom_call" | custom-call | tf_op jit(solution)/shard_map/pallas_call | solution.py:775
  66.0 2.3 %shard_map.172 = (bf16[197,2,768]{2,1,0:T(2,128)(2,1)}, f32[197,2,768]{2,1,0:T(2,128)}, f32[50,2,384]{2,1,0:T(2,128)}, f32[1,1]{1,0:T(1,128)}, f32[50,2,384]{2,1...) custom-call(bf16[6,200,2,128]{3,2,1,0:T(2,128)(2,1)S(1)} %get-tuple-element.21.refs_0_, ...), custom_call_target="tpu_custom_call" | custom-call | tf_op jit(solution)/shard_map/pallas_call | solution.py:702

commit v3 on v2

--- a/solution.py
+++ b/solution.py
@@ -116,6 +116,7 @@
     NJ = D // 128
     HJ = NJ // 2
     PB = 16
+    M = B * TK
     core = lax.axis_index("mlp")
     other = 1 - core
     me = lax.axis_index("dp")
@@ -236,7 +237,7 @@
 
     def spread(src_v, store):
         for j in range(NJ):
-            stage_v[j, 0 : T * B] = src_v[j, 0 : T * B].astype(F32)
+            stage_v[j] = src_v[j].astype(F32)
         for b in range(B):
             for j in range(NJ):
                 store(b, slice(128 * j, 128 * (j + 1)), stage_v[j, pl.ds(b, T, stride=B), :])
@@ -275,9 +276,9 @@
         return place.at[rows : rows + TQ, cols : cols + S]
 
     def attend_forward(l):
-        def image(b, carry):
-            qr = pl.ds(pl.multiple_of(b * TQ, 16), TQ)
-            kr = pl.ds(pl.multiple_of(b * S, 16), S)
+        for b in range(B):
+            qr = slice(b * TQ, (b + 1) * TQ)
+            kr = slice(b * S, (b + 1) * S)
             for hp in range(H // 2):
                 sl = slice(2 * HD * hp, 2 * HD * (hp + 1))
                 q = q_s[l, qr, sl]
@@ -301,9 +302,6 @@
                 inv = pltpu.roll(1.0 / total, HD, 1)
                 ri_s[l, qr, sl] = inv.astype(BF16)
                 o_s[l, qr, sl] = (top_part * inv).astype(BF16)
-            return carry
-
-        lax.fori_loop(0, B, image, 0)
 
     def back_half(l, b, hp, part, first):
         at = pl.multiple_of(hp * 2 * HD, 2 * HD)
@@ -439,7 +437,7 @@
     def mlp_chunk(l, part, j, last_):
         cols = slice(j * C, (j + 1) * C)
         at = slice((part * (FH // C) + j) * C, (part * (FH // C) + j + 1) * C)
-        pre = mm(x16[...], w_up[l, part, :, cols]) + ub[part, pl.ds(l, 1), cols]
+        pre = mm(x16[0:M, :], w_up[l, part, :, cols]) + ub[part, pl.ds(l, 1), cols]
         cdf = 0.5 + 0.5 * lax.erf(pre * 0.7071067811865476)
         if last_ != "output":
             bell = jnp.exp2(pre * pre * (-0.5 * LOG2E)) * 0.3989422804014327
@@ -447,9 +445,9 @@
         if last_ != "slope":
             add = mm((pre * cdf).astype(BF16), w_dn[l, part, cols, :])
             if part == 0 and j == 0:
-                acc[...] = add
+                acc[0:M, :] = add
             else:
-                acc[...] += add
+                acc[0:M, :] += add
 
     chunks = [(part, j) for part in range(2) for j in range(FH // C)]
 
@@ -475,12 +473,12 @@
     def norm_two(l):
         branch = mm(o_s[l], w_out[l]) + bias[l, 2:3, :]
         for b in range(B):
-            hid[b * TQ : (b + 1) * TQ, :] = seq[b, 0:TQ, :] + branch[b * TQ : (b + 1) * TQ]
+            hid[b * TK : (b + 1) * TK, :] = seq[b, 0:TK, :] + branch[b * TQ : b * TQ + TK]
         gain2, shift2 = norms[l, 2:3, :], norms[l, 3:4, :]
-        xh, inv = norm_rows(hid[...])
+        xh, inv = norm_rows(hid[0:M, :])
         xh2[l] = xh.astype(BF16)
-        inv_s[l, 0 : B * TQ, 1:2] = inv
-        x16[...] = (xh * gain2 + shift2).astype(BF16)
+        inv_s[l, 0:M, 1:2] = inv
+        x16[0:M, :] = (xh * gain2 + shift2).astype(BF16)
 
     norm_one(0)
     copy_weight(0, 0).wait()
@@ -514,8 +512,8 @@
                     push_weight(l, 1).wait()
                 mlp_chunk(l, part, j, "both")
             for b in range(B):
-                at = slice(b * TQ, (b + 1) * TQ)
-                seq[b, 0:TQ, :] = hid[at, :] + acc[at, :] + bias[l, 3:4, :]
+                at = slice(b * TK, (b + 1) * TK)
+                seq[b, 0:TK, :] = hid[at, :] + acc[at, :] + bias[l, 3:4, :]
             norm_one(l + 1)
             copy_weight(l + 1, 0).wait()
 
@@ -530,21 +528,21 @@
     for part, j in chunks:
         mlp_chunk(L - 1, part, j, "slope")
     for b in range(B):
-        seq[b, 0:TQ, :] = hid[b * TQ : (b + 1) * TQ, :] + bias[L - 1, 3:4, :]
+        seq[b, 0:TK, :] = hid[b * TK : (b + 1) * TK, :] + bias[L - 1, 3:4, :]
 
     def activations_out():
         for b in range(B):
-            seq[b, 0:TQ, :] += acc[b * TQ : (b + 1) * TQ, :]
+            seq[b, 0:TK, :] += acc[b * TK : (b + 1) * TK, :]
             for j in range(NJ):
                 stage_v[j, pl.ds(b, T, stride=B), :] = seq[b, 0:T, 128 * j : 128 * (j + 1)]
         for j in range(NJ):
-            tok_v[j, 0 : T * B] = stage_v[j, 0 : T * B].astype(BF16)
+            tok_v[j] = stage_v[j].astype(BF16)
 
     for b in range(B):
-        hid[b * TQ + TK - 8 : (b + 1) * TQ, :] = jnp.zeros((TQ - TK + 8, D), F32)
+        hid[(b + 1) * TK - 8 : (b + 1) * TK, :] = jnp.zeros((8, D), F32)
 
     def store_cot(b, cols, rows):
-        hid[b * TQ : b * TQ + T, cols] = rows
+        hid[b * TK : b * TK + T, cols] = rows
 
     spread(cot_v, store_cot)
 
@@ -556,25 +554,28 @@
             pl.when(step > 0)(lambda: phase(above))
 
         sum_above(reduce_group)
-        x16[...] = hid[...].astype(BF16)
+        x16[0:M, :] = hid[0:M, :].astype(BF16)
         for part in range(2):
             for j in range(FH // C):
                 cols = slice(j * C, (j + 1) * C)
                 at = slice((part * (FH // C) + j) * C, (part * (FH // C) + j + 1) * C)
-                ga = mm_nt(x16[...], w_dn[l, part, cols, :])
+                ga = mm_nt(x16[0:M, :], w_dn[l, part, cols, :])
                 gpre = (gp_s[l, :, at].astype(F32) * ga).astype(BF16)
                 add = mm_nt(gpre, w_up[l, part, :, cols])
                 if part == 0 and j == 0:
-                    acc[...] = add
+                    acc[0:M, :] = add
                 else:
-                    acc[...] += add
+                    acc[0:M, :] += add
         gain2 = norms[l, 2:3, :]
 
-        new = hid[...] + ln_back(
-            acc[...], xh2[l].astype(F32), inv_s[l, 0 : B * TQ, 1:2], gain2
+        new = hid[0:M, :] + ln_back(
+            acc[0:M, :], xh2[l].astype(F32), inv_s[l, 0:M, 1:2], gain2
         )
-        hid[...] = new
-        x16[...] = mm_nt(new.astype(BF16), w_out[l]).astype(BF16)
+        hid[0:M, :] = new
+        grad_mixed = mm_nt(new.astype(BF16), w_out[l])
+        for b in range(B):
+            rows = [grad_mixed[b * TK : (b + 1) * TK], jnp.zeros((TQ - TK, D), F32)]
+            x16[b * TQ : (b + 1) * TQ, :] = jnp.concatenate(rows, axis=0).astype(BF16)
         gain = norms[l, 0:1, :]
 
         def high_keys(b, hp):
@@ -610,9 +611,9 @@
         pl.when(l == 0)(lambda: reduce_group(l))
         sum_above(reduce_end)
         for b in range(B):
-            at = slice(b * TQ, b * TQ + TK)
+            at = slice(b * TK, (b + 1) * TK)
             dx = ln_back(
-                acc[at, :],
+                acc[b * TQ : b * TQ + TK, :],
                 xh1[l, b * S : b * S + TQ, :].astype(F32)[:TK],
                 inv_s[l, b * S : b * S + TK, 0:1],
                 gain,
@@ -624,7 +625,7 @@
     for j in range(HJ):
         copy_moment(0, j).start()
         copy_moment(1, j).start()
-    x16[...] = (xh2[L - 1].astype(F32) * norms[L - 1, 2:3, :] + norms[L - 1, 3:4, :]).astype(BF16)
+    x16[0:M, :] = (xh2[L - 1].astype(F32) * norms[L - 1, 2:3, :] + norms[L - 1, 3:4, :]).astype(BF16)
     for i, (part, j) in enumerate(chunks):
         if i == len(chunks) - 2:
             reduce_ranks(0)
@@ -633,7 +634,7 @@
     for j in range(NJ):
         for b in range(B):
             stage_v[j, pl.ds(b, T, stride=B), :] = hid[
-                b * TQ : b * TQ + T, 128 * j : 128 * (j + 1)
+                b * TK : b * TK + T, 128 * j : 128 * (j + 1)
             ]
     reduce_end(0)
 
@@ -746,7 +747,7 @@
         VMEM((B * S, 3 * D), BF16),
         VMEM((B * TQ, D), BF16),
         VMEM((L, B * S, D), BF16),
-        VMEM((L, B * TQ, D), BF16),
+        VMEM((L, B * TK, D), BF16),
         VMEM((L, B * S, 2), F32),
         VMEM((L, B * TQ, D), BF16),
         VMEM((L, B * S, D), BF16),
@@ -754,7 +755,7 @@
         VMEM((L, B, H, TQ, S), BF16),
         VMEM((L, B * TQ, D), BF16),
         VMEM((L, B * TQ, D), BF16),
-        VMEM((L, B * TQ, 2 * FH), BF16),
+        VMEM((L, B * TK, 2 * FH), BF16),
         VMEM((L, 2 * G, HJ, PB, 128), BF16),
         VMEM((L, 2 * G, HJ, PB, 128), BF16),
         VMEM((L, R, HJ, PB, 128), BF16),

time: 68.6 us -> 66.1 us (0.964)
  Pallas kernels: 67.7 us -> 65.1 us
    pallas_call x1, Pallas kernels: 65.4 us -> 62.9 us  [local(): pl.pallas_call(functools.partial(main_kernel, dims), out_shape=(VMEM((NJ,...]
where the time goes in v3:
time: 66.1 us; the launch traced here: 66 us
  Pallas kernels  65.1 us (98%)
  between operations  0.83 us (1%)
    pallas_call x1, Pallas kernels, local(): pl.pallas_call(functools.partial(main_kernel, dims), out_shape=(VMEM((NJ,...  62.9 us
    pallas_call x1, Pallas kernels, hand_on(): pl.pallas_call(hand_on_kernel, out_shape=tuple((whole(a, rows) for a, row...  2.26 us

profile of v3, /device:TPU:0, one launch (start us, length us, event | category | flops | bytes accessed | tf_op | source)
XLA Modules:
  0.0 66.0 jit_solution(15979807730894187625)
XLA Ops:
  0.6 62.9 %shard_map.171 = (bf16[6,200,2,128]{3,2,1,0:T(2,128)(2,1)S(1)}, f32[6,200,2,128]{3,2,1,0:T(2,128)S(1)}, f32[3,56,2,128]{3,2,1,0:T(2,128)S(1)}, f32[1,1]{1,0:T(1,...) custom-call(bf16[197,2,768]{2,1,0:T(2,128)(2,1)} %bitcast.12, ...), custom_call_target="tpu_custom_call" | custom-call | tf_op jit(solution)/shard_map/pallas_call | solution.py:776
  63.5 2.3 %shard_map.172 = (bf16[197,2,768]{2,1,0:T(2,128)(2,1)}, f32[197,2,768]{2,1,0:T(2,128)}, f32[50,2,384]{2,1,0:T(2,128)}, f32[1,1]{1,0:T(1,128)}, f32[50,2,384]{2,1...) custom-call(bf16[6,200,2,128]{3,2,1,0:T(2,128)(2,1)S(1)} %get-tuple-element.21.refs_0_, ...), custom_call_target="tpu_custom_call" | custom-call | tf_op jit(solution)/shard_map/pallas_call | solution.py:703

commit v4 on v3

--- a/solution.py
+++ b/solution.py
@@ -47,6 +47,14 @@
         return carry
 
     lax.fori_loop(0, count // step, one, 0, unroll=unroll)
+
+
+def square_of(block):
+    block = block.astype(F32)
+    total = block[0] * block[0]
+    for j in range(1, block.shape[0]):
+        total += block[j] * block[j]
+    return total
 
 
 def main_kernel(
@@ -65,8 +73,8 @@
     dn_hbm,
     tok_nat,
     stage_nat,
-    grad_nat,
-    norm_s,
+    sums_out,
+    squares_out,
     first_nat,
     second_nat,
     prompt_nat,
@@ -405,13 +413,6 @@
         lax.fori_loop(1, R, go, 0, unroll=R <= 4)
         all_of(part_h, l, 2 * G - 1, sem_b).wait_send()
 
-    def square_of(block):
-        block = block.astype(F32)
-        total = block[0] * block[0]
-        for j in range(1, HJ):
-            total += block[j] * block[j]
-        return total
-
     def reduce_ranks(l):
         if R > 1:
             all_of(slot_c, l, R - 1, sem_c).wait_recv()
@@ -636,77 +637,105 @@
             stage_v[j, pl.ds(b, T, stride=B), :] = hid[
                 b * TK : b * TK + T, 128 * j : 128 * (j + 1)
             ]
+    for j in range(HJ):
+        prompt_nat[j] = prom_nat[core * HJ + j]
+        copy_moment(0, j).wait()
+        copy_moment(1, j).wait()
     reduce_end(0)
-
-    grad_v = grad_nat.reshape(HJ, PP * L, 128)
+    sums_out[...] = fin[...]
+    squares_out[...] = sq_in[...]
+
+
+def finish_kernel(
+    act, igrad, sums, theirs, first, second, prompt,
+    act_hbm, igrad_hbm, grad_hbm, norm_hbm, first_hbm, second_hbm, prompt_hbm,
+    grad, norm, new_first, new_second, new_prompt, sem,
+):
+    leaving = []
+
+    def leave(src, dst):
+        copy = pltpu.make_async_copy(src, dst, sem.at[len(leaving)])
+        copy.start()
+        leaving.append(copy)
+
+    def columns_out(src, dst, j):
+        leave(src.at[j, 0 : dst.shape[0]], dst.at[:, :, 128 * j : 128 * (j + 1)])
+
+    for src, dst in ((igrad, igrad_hbm), (act, act_hbm)):
+        for j in range(src.shape[0]):
+            columns_out(src, dst, j)
+    L, G, HJ, PB, _ = sums.shape
+    PP = grad.shape[1]
+    n = grad_hbm.shape[0] * L
+    flat = (HJ, PP * L, 128)
+    grad_v = grad.reshape(*flat)
     for l in range(L):
         for k in range(G):
-            rows = min(PB, PN - k * PB)
+            rows = min(PB, n // L - k * PB)
             for j in range(HJ):
-                grad_v[j, pl.ds(k * PB * L + l, rows, stride=L), :] = fin[l, k, j].astype(F32)[:rows]
-    n = PN * L
-    own, theirs = jnp.zeros((PB, 128), F32), jnp.zeros((PB, 128), F32)
+                grad_v[j, pl.ds(k * PB * L + l, rows, stride=L), :] = sums[l, k, j].astype(F32)[
+                    :rows
+                ]
+    for j in range(HJ):
+        columns_out(grad, grad_hbm, j)
+    own_sum, other_sum = jnp.zeros((PB, 128), F32), jnp.zeros((PB, 128), F32)
     for l in range(L):
         for k in range(G):
-            own += square_of(fin[l, k])
-            theirs += sq_in[l, k]
-    squares = jnp.sum(own + theirs, axis=(0, 1), keepdims=True)
-    grad_norm = jnp.sqrt(squares)
-    norm_s[...] = grad_norm
+            own_sum += square_of(sums[l, k])
+            other_sum += theirs[l, k]
+    grad_norm = jnp.sqrt(jnp.sum(own_sum + other_sum, axis=(0, 1), keepdims=True))
+    norm[...] = grad_norm
+    leave(norm, norm_hbm)
     factor = jnp.minimum(1.0, clip_limit / (grad_norm + 1e-06))
     fix_first = 1.0 - beta_one**STEP
     fix_second = 1.0 - beta_two**STEP
     for j in range(HJ):
-        copy_moment(0, j).wait()
-        copy_moment(1, j).wait()
-        first_v = first_nat.reshape(HJ, PP * L, 128)
-        second_v = second_nat.reshape(HJ, PP * L, 128)
-        prompt_v = prompt_nat.reshape(HJ, PP * L, 128)
         clipped = grad_v[j, 0:n, :] * factor
-        new_first = beta_one * first_v[j, 0:n, :] + (1.0 - beta_one) * clipped
-        new_second = beta_two * second_v[j, 0:n, :] + (1.0 - beta_two) * clipped * clipped
-        first_v[j, 0:n, :] = new_first
-        second_v[j, 0:n, :] = new_second
-        old = prom_v[core * HJ + j, 0:n, :]
-        prompt_v[j, 0:n, :] = old - learn_rate * (
-            new_first / fix_first / (jnp.sqrt(new_second / fix_second) + adam_eps)
+        up_first = beta_one * first.reshape(*flat)[j, 0:n, :] + (1.0 - beta_one) * clipped
+        up_second = (
+            beta_two * second.reshape(*flat)[j, 0:n, :] + (1.0 - beta_two) * clipped * clipped
+        )
+        new_first.reshape(*flat)[j, 0:n, :] = up_first
+        new_second.reshape(*flat)[j, 0:n, :] = up_second
+        old = prompt.reshape(*flat)[j, 0:n, :]
+        new_prompt.reshape(*flat)[j, 0:n, :] = old - learn_rate * (
+            up_first / fix_first / (jnp.sqrt(up_second / fix_second) + adam_eps)
             + weight_decay * old
         )
-
-
-def hand_on_kernel(*refs):
-    n = (len(refs) - 1) // 2
-    sources, targets, sem = refs[:n], refs[n : 2 * n], refs[2 * n]
-    copies = []
-    for src, dst in zip(sources, targets):
-        if len(src.shape) == 2:
-            copies.append(pltpu.make_async_copy(src, dst, sem.at[len(copies)]))
-        else:
-            rows = dst.shape[0]
-            for j in range(src.shape[0]):
-                view = dst.at[:, :, 128 * j : 128 * (j + 1)]
-                copies.append(
-                    pltpu.make_async_copy(src.at[j, 0:rows], view, sem.at[len(copies)])
-                )
-    for copy in copies:
-        copy.start()
-    for copy in copies:
+        columns_out(new_first, first_hbm, j)
+        columns_out(new_second, second_hbm, j)
+        columns_out(new_prompt, prompt_hbm, j)
+    for copy in leaving:
         copy.wait()
 
 
-def hand_on(arrays, counts):
-    def whole(a, rows):
-        shape = a.shape if len(a.shape) == 2 else (rows, a.shape[2], a.shape[0] * a.shape[3])
-        return jax.ShapeDtypeStruct(shape, a.dtype)
-
-    copies = sum(1 if len(a.shape) == 2 else a.shape[0] for a in arrays)
+def finish(arrays, T, PN):
+    act, igrad, _, _, first, _, _ = arrays
+    HJ, PP, L, _ = first.shape
+    small = jax.ShapeDtypeStruct((PN, L, HJ * 128), F32)
+    big = (T, act.shape[2], act.shape[0] * 128)
     return pl.pallas_call(
-        hand_on_kernel,
-        out_shape=tuple(whole(a, rows) for a, rows in zip(arrays, counts)),
+        finish_kernel,
+        out_shape=(
+            jax.ShapeDtypeStruct(big, act.dtype),
+            jax.ShapeDtypeStruct(big, igrad.dtype),
+            small,
+            jax.ShapeDtypeStruct((1, 1), F32),
+            small,
+            small,
+            small,
+        ),
         in_specs=[pl.BlockSpec(memory_space=VMEM)] * len(arrays),
-        out_specs=(pl.BlockSpec(memory_space=pl.ANY),) * len(arrays),
-        scratch_shapes=[DMA((copies,))],
-        compiler_params=pltpu.CompilerParams(vmem_limit_bytes=2**20),
+        out_specs=(pl.BlockSpec(memory_space=pl.ANY),) * 7,
+        scratch_shapes=[
+            VMEM(first.shape, F32),
+            VMEM((1, 1), F32),
+            VMEM(first.shape, F32),
+            VMEM(first.shape, F32),
+            VMEM(first.shape, F32),
+            DMA((2 * act.shape[0] + 4 * HJ + 1,)),
+        ],
+        compiler_params=pltpu.CompilerParams(vmem_limit_bytes=2 * 2**20),
     )(*arrays)
 
 
@@ -778,8 +807,8 @@
         out_shape=(
             VMEM((NJ, TK, B, 128), BF16),
             VMEM((NJ, TK, B, 128), F32),
-            small,
-            VMEM((1, 1), F32),
+            VMEM((L, G, HJ, PB, 128), BF16),
+            VMEM((L, G, PB, 128), F32),
             small,
             small,
             small,
@@ -794,9 +823,7 @@
         native(second_moment), norm_params, bias_rows, qkv_weight, out_weight,
         up_weight, up_bias, down_weight,
     )
-    act, igrad, grad, norm, new_first, new_second, new_prompts = hand_on(
-        results, (T, T, PN, 1, PN, PN, PN)
-    )
+    act, igrad, grad, norm, new_first, new_second, new_prompts = finish(results, T, PN)
     return (
         native(act), native(igrad), native(grad), norm.reshape(()),
         native(new_first), native(new_second), native(new_prompts),

time: 66.1 us -> 64.7 us (0.979)
  Pallas kernels: 65.1 us -> 63.7 us
    pallas_call x1, Pallas kernels: 62.9 us -> 62.1 us  [local(): pl.pallas_call(functools.partial(main_kernel, dims), out_shape=(VMEM((NJ,...]
where the time goes in v4:
time: 64.7 us; the launch traced here: 64.5 us
  Pallas kernels  63.7 us (98%)
  between operations  0.83 us (1%)
    pallas_call x1, Pallas kernels, local(): pl.pallas_call(functools.partial(main_kernel, dims), out_shape=(VMEM((NJ,...  62.1 us
    pallas_call x1, Pallas kernels, finish(): pl.pallas_call(finish_kernel, out_shape=(jax.ShapeDtypeStruct(big, act.dt...  1.64 us

profile of v4, /device:TPU:0, one launch (start us, length us, event | category | flops | bytes accessed | tf_op | source)
XLA Modules:
  0.0 64.5 jit_solution(5750186650165095635)
XLA Ops:
  0.6 62.1 %shard_map.171 = (bf16[6,200,2,128]{3,2,1,0:T(2,128)(2,1)S(1)}, f32[6,200,2,128]{3,2,1,0:T(2,128)S(1)}, bf16[2,4,3,16,128]{4,3,2,1,0:T(8,128)(2,1)S(1)}, f32[2,4...) custom-call(bf16[197,2,768]{2,1,0:T(2,128)(2,1)} %bitcast.12, ...), custom_call_target="tpu_custom_call" | custom-call | tf_op jit(solution)/shard_map/pallas_call | solution.py:805
  62.7 1.6 %shard_map.172 = (bf16[197,2,768]{2,1,0:T(2,128)(2,1)}, f32[197,2,768]{2,1,0:T(2,128)}, f32[50,2,384]{2,1,0:T(2,128)}, f32[1,1]{1,0:T(1,128)}, f32[50,2,384]{2,1...) custom-call(bf16[6,200,2,128]{3,2,1,0:T(2,128)(2,1)S(1)} %get-tuple-element.21.act, ...), custom_call_target="tpu_custom_call" | custom-call | tf_op jit(solution)/shard_map/pallas_call | solution.py:717

commit v5 on v4

--- a/solution.py
+++ b/solution.py
@@ -356,8 +356,8 @@
         kr = pl.ds(pl.multiple_of(b * S, 16), S)
         k = k_s[l, kr, sl]
         zero = jnp.zeros_like(k)
-        dq = mm(jnp.concatenate([low[:, :SH], high[0]], axis=1), jnp.where(even_k, k, zero))
-        dq += mm(jnp.concatenate([low[:, SH:], high[1]], axis=1), jnp.where(even_k, zero, k))
+        both = jnp.concatenate([jnp.where(even_k, k, zero), jnp.where(even_k, zero, k)], axis=0)
+        dq = mm(jnp.concatenate([low[:, :SH], high[0], low[:, SH:], high[1]], axis=1), both)
         wide[pl.ds(pl.multiple_of(b * S, 16), TQ), sl] = (dq * scale).astype(BF16)
 
     def pairs_loop(body, lo, hi):
@@ -391,7 +391,7 @@
             for k in range(G):
                 block = rows[k * PB : (k + 1) * PB, 128 * j : 128 * (j + 1)]
                 part_h[l, j // HJ * G + k, j % HJ] = block.astype(BF16)
-        for k, c in around:
+        for k, c in reversed(around):
             to = lax.rem(core + c, 2) * G + member(k)
             send(
                 part_h.at[l, to], slot_b.at[l, mine_b], sem_b, l, neighbour(k, c)
@@ -482,10 +482,12 @@
         x16[0:M, :] = (xh * gain2 + shift2).astype(BF16)
 
     norm_one(0)
-    copy_weight(0, 0).wait()
     copy_small(2).start()
     for i in range(1, 4):
         copy_weight(0, i).start()
+    for j in range(NJ):
+        copy_cot(j).start()
+    copy_weight(0, 0).wait()
 
     def forward(l, carry):
         attend(l)
@@ -499,8 +501,6 @@
                     push_weight(later, i).start()
                 for i in range(4):
                     copy_weight(later, i).start()
-            for j in range(NJ):
-                copy_cot(j).start()
             copy_small(2).wait()
             push_ub().wait()
 

time: 64.7 us -> 64.6 us (level)
  no operation moved by 1% of the time
where the time goes in v5:
time: 64.6 us; the launch traced here: 64.5 us
  Pallas kernels  63.7 us (99%)
  between operations  0.83 us (1%)
    pallas_call x1, Pallas kernels, local(): pl.pallas_call(functools.partial(main_kernel, dims), out_shape=(VMEM((NJ,...  62 us
    pallas_call x1, Pallas kernels, finish(): pl.pallas_call(finish_kernel, out_shape=(jax.ShapeDtypeStruct(big, act.dt...  1.64 us

profile of v5, /device:TPU:0, one launch (start us, length us, event | category | flops | bytes accessed | tf_op | source)
XLA Modules:
  0.0 64.5 jit_solution(1782743158058974824)
XLA Ops:
  0.6 62.0 %shard_map.171 = (bf16[6,200,2,128]{3,2,1,0:T(2,128)(2,1)S(1)}, f32[6,200,2,128]{3,2,1,0:T(2,128)S(1)}, bf16[2,4,3,16,128]{4,3,2,1,0:T(8,128)(2,1)S(1)}, f32[2,4...) custom-call(bf16[197,2,768]{2,1,0:T(2,128)(2,1)} %bitcast.12, ...), custom_call_target="tpu_custom_call" | custom-call | tf_op jit(solution)/shard_map/pallas_call | solution.py:805
  62.7 1.6 %shard_map.172 = (bf16[197,2,768]{2,1,0:T(2,128)(2,1)}, f32[197,2,768]{2,1,0:T(2,128)}, f32[50,2,384]{2,1,0:T(2,128)}, f32[1,1]{1,0:T(1,128)}, f32[50,2,384]{2,1...) custom-call(bf16[6,200,2,128]{3,2,1,0:T(2,128)(2,1)S(1)} %get-tuple-element.21.act, ...), custom_call_target="tpu_custom_call" | custom-call | tf_op jit(solution)/shard_map/pallas_call | solution.py:717
